TPU v7x, 32 devices: a whole 2x2x4 slice. The times are simulated.
32 devices in a mesh: dp: 4 (over y, x), vocab: 8 (over z, core).
Axes of the slice: x: 2, y: 2, z: 4, core: 2. Of those that a mesh axis runs over, the one named last changes fastest.
Arguments:
- query_hidden: bfloat16 [8, 128, 4096], P('dp', None, 'vocab'), may hold values from -144 to 144
- passage_hidden: bfloat16 [8, 256, 4096], P('dp', None, 'vocab'), may hold values from -144 to 144
- head_weight: bfloat16 [4096, 16384], P(None, 'vocab'), may hold values from -6 to 6
- query_mask: int32 [8, 128], P('dp'), may hold values from 0 to 1, as said below
- passage_mask: int32 [8, 256], P('dp'), may hold values from 0 to 1, as said below
- positive: int32 [8], replicated, may hold values from 0 to 7
Outputs:
- grad_query_hidden: bfloat16 [8, 128, 4096], P('dp', None, 'vocab')
- grad_passage_hidden: bfloat16 [8, 256, 4096], P('dp', None, 'vocab')
- query_loss: float32 [8], P('dp')
Inputs may be any that keep to these rules, and one draw needn't show every extreme that they name: `query_mask`: the live tokens of each query are a prefix of 32 to 128 positions. `passage_mask`: the live tokens of each passage are a prefix of 64 to 256 positions.
All inputs are finite; a program needn't handle non-finite values.
Results may differ from a plain program's by a relative error of at most 0.0095.
Values may be sent and summed in bfloat16 or wider, within the bound.
A program may use at most 128 MiB of HBM per device.

v0:
```python
import jax
import jax.numpy as jnp
from jax import lax
from jax.sharding import PartitionSpec as P

normalizer_sharpness = 0.2
score_div = 16.0
loss_scale = 65536.0


def pooling_row_block(lexicon_projection_lines, live):
    divided_similarity_matrix = lexicon_projection_lines / normalizer_sharpness
    live_rows = live[:, :, None] > 0
    largest_element = jnp.max(jnp.where(live_rows, divided_similarity_matrix, -1e30), axis=1)
    expo = jnp.where(
        live_rows, jnp.exp(divided_similarity_matrix - largest_element[:, None, :]), 0.0
    )
    cumulative_accumulator = jnp.sum(expo, axis=1)
    softened_rectifier_output = normalizer_sharpness * (
        largest_element + jnp.log(cumulative_accumulator)
    )
    return (softened_rectifier_output, expo / cumulative_accumulator[:, None, :])


def exact_dot(left, right):
    return jnp.dot(left, right, precision=lax.Precision.HIGHEST, preferred_element_type=jnp.float32)


def loss_and_grad(scores, targets, total_queries):
    largest_element = jnp.max(scores, axis=1)
    lse = largest_element + jnp.log(jnp.sum(jnp.exp(scores - largest_element[:, None]), axis=1))
    picked = (targets[:, None] == jnp.arange(scores.shape[1], dtype=jnp.int32)[None, :]).astype(
        jnp.float32
    )
    losses = lse - jnp.sum(scores * picked, axis=1)
    probs = jnp.exp(scores - lse[:, None])
    return (losses, (probs - picked) * (loss_scale / total_queries))


def token_grads(dpooled, softened_rectifier_output, share):
    dsmooth = dpooled * jnp.where(
        softened_rectifier_output > 0,
        1.0 / (1.0 + jnp.maximum(softened_rectifier_output, 0.0)),
        0.0,
    )
    dlogits = (share * dsmooth[:, None, :]).astype(jnp.bfloat16)
    return dlogits.reshape(dlogits.shape[0] * dlogits.shape[1], dlogits.shape[2])


def on_device(query_hidden, passage_hidden, head_weight, query_mask, passage_mask, positive):
    q_count, q_len, width_part = query_hidden.shape
    p_count, p_len, _ = passage_hidden.shape
    columns = head_weight.shape[1]
    split = q_count * q_len
    tokens = jnp.concatenate(
        [
            query_hidden.reshape(split, width_part),
            passage_hidden.reshape(p_count * p_len, width_part),
        ],
        axis=0,
    )
    w_rows = head_weight
    lexicon_projection_lines = jnp.dot(
        lax.all_gather(tokens, "vocab", axis=1, tiled=True),
        w_rows,
        preferred_element_type=jnp.float32,
    )
    q_smooth, q_share = pooling_row_block(
        lexicon_projection_lines[:split].reshape(q_count, q_len, columns), query_mask
    )
    p_smooth, p_share = pooling_row_block(
        lexicon_projection_lines[split:].reshape(p_count, p_len, columns), passage_mask
    )
    q_pooled = jnp.log1p(jnp.maximum(q_smooth, 0.0))
    p_pooled = jnp.log1p(jnp.maximum(p_smooth, 0.0))
    group = lax.axis_index("dp")
    total_queries = positive.shape[0]
    p_every = lax.all_gather(p_pooled, "dp", axis=0, tiled=True)
    scores = lax.psum(exact_dot(q_pooled, p_every.T), "vocab") / score_div
    targets = lax.dynamic_slice_in_dim(positive, group * q_count, q_count, 0)
    query_loss, dscores = loss_and_grad(scores, targets, total_queries)
    dq_pooled = exact_dot(dscores, p_every) / score_div
    grad_passage_summary = lax.psum_scatter(
        exact_dot(dscores.T, q_pooled) / score_div, "dp", scatter_dimension=0, tiled=True
    )
    dlogits = jnp.concatenate(
        [
            token_grads(dq_pooled, q_smooth, q_share),
            token_grads(grad_passage_summary, p_smooth, p_share),
        ],
        axis=0,
    )
    w_rows = head_weight
    own_grad = lax.psum_scatter(
        lax.dot_general(
            w_rows, dlogits, (((1,), (1,)), ((), ())), preferred_element_type=jnp.float32
        ),
        "vocab",
        scatter_dimension=0,
        tiled=True,
    ).T
    own_grad = own_grad.astype(jnp.bfloat16)
    grad_query_hidden = own_grad[:split].reshape(q_count, q_len, width_part)
    grad_passage_hidden = own_grad[split:].reshape(p_count, p_len, width_part)
    return (grad_query_hidden, grad_passage_hidden, query_loss)


def solution(mesh):
    return jax.shard_map(
        on_device,
        mesh=mesh,
        in_specs=(
            P("dp", None, "vocab"),
            P("dp", None, "vocab"),
            P(None, "vocab"),
            P("dp", None),
            P("dp", None),
            P(),
        ),
        out_specs=(P("dp", None, "vocab"), P("dp", None, "vocab"), P("dp")),
        check_vma=False,
    )
```

profile of v0, /device:TPU:0, one launch (start us, length us, event | category | flops | bytes accessed | tf_op | source)
XLA Modules:
  0.0 323.6 jit_solution(504637239157249309)
XLA Ops:
  7.2 2.1 pad_maximum_fusion
  9.4 0.7 broadcast_compare_fusion
  10.1 1.2 dynamic-slice
  12.0 0.7 dynamic_slice.3
  12.8 0.7 broadcast_compare_fusion.1
  13.4 0.7 fusion.29
  14.1 62.9 %all-gather.3.cloned.1.call-done = bf16[768,4096]{1,0:T(8,128)(2,1)} async-done(((bf16[768,512]{1,0:T(8,128)(2,1)}), bf16[768,4096]{1,0:T(8,128)(2,1)}) %all-gather.3.cloned.1.call-update) | async-done | bytes 6291472 | tf_op jit(solution)/shard_map/all_gather | solution.py:64
  77.1 17.7 %fusion.23 = f32[768,2048]{1,0:T(8,128)S(1)} fusion(bf16[768,4096]{1,0:T(8,128)(2,1)} %all-gather.3.cloned.1.call-done, bf16[4096,2048]{1,0:T(8,128)(2,1)} %param.8), kind=kOutput, calls=%fused_computation.53 | convolution fusion | flops 12884901888 | bytes 29360128 | tf_op jit(solution)/shard_map/dot_general | solution.py:63
  94.8 0.6 select_reduce_fusion.1
  96.2 1.2 copy-done
  97.5 0.9 select_reduce_fusion
  98.4 8.2 %all-gather = f32[4,2,2048]{2,1,0:T(2,128)S(1)} all-gather(f32[1,2,2048]{2,1,0:T(2,128)S(1)} %log-plus-one_bitcast_fusion), channel_id=1, replica_groups=mesh['dp'=4,'vocab'=8] {'dp'}, dimensions={0}, use_global_device_ids=true | all-gather | bytes 81920 | tf_op jit(solution)/shard_map/all_gather | solution.py:78
  106.9 13.6 %psum.7 = f32[2,8]{1,0:T(2,128)S(1)} all-reduce(f32[2,8]{1,0:T(2,128)S(1)} %fusion.12), channel_id=1, replica_groups=mesh['dp'=4,'vocab'=8] {'vocab'}, use_global_device_ids=true, to_apply=%region_4.5 | all-reduce | flops 16 | bytes 128 | tf_op jit(solution)/shard_map/psum | solution.py:79
  120.9 0.5 fusion.22
  121.4 1.0 convolution_multiply_fusion
  122.9 2.2 fusion.7
  125.1 36.2 %all-reduce.3.cloned.1.call-done = f32[8,2048]{1,0:T(8,128)} async-done(((f32[8,2048]{1,0:T(8,128)}), f32[8,2048]{1,0:T(8,128)}) %all-reduce.3.cloned.1.call-update) | async-done | bytes 65552
  161.3 0.9 fusion.10
  162.2 3.0 fusion
  165.1 19.4 %convolution_bitcast_fusion = f32[4096,768]{0,1:T(8,128)} fusion(bf16[4096,2048]{1,0:T(8,128)(2,1)} %param.8, bf16[512,2048]{1,0:T(8,128)(2,1)S(1)} %fusion, bf16[256,2048]{1,0:T(8,128)(2,1)S(1)} %fusion.7), kind=kOutput, calls=%fused_computation | convolution fusion | flops 12891193344 | bytes 32505856 | tf_op jit(solution)/shard_map/dot_general | solution.py:95
  184.6 129.4 %reduce-scatter.2.cloned.1.call-done = f32[512,768]{0,1:T(8,128)} async-done(((f32[4096,768]{0,1:T(8,128)}), f32[512,768]{0,1:T(8,128)}) %reduce-scatter.2.cloned.1.call-update) | async-done | bytes 1572880 | tf_op jit(solution)/shard_map/reduce_scatter | solution.py:94
  314.0 1.5 convert_bitcast_fusion
  315.5 0.7 slice.18
  316.2 0.8 slice.19
  (16 shorter events, 2.1 us)
Async XLA Ops:
  7.2 69.9 %all-gather.3.cloned.1.call-start = ((), (), s32[]{:S(2)}) async-start(), calls=%async_computation.1 | async-start | bytes 7077888 | tf_op jit(solution)/shard_map/all_gather | solution.py:64
  9.4 151.9 %all-reduce.3.cloned.1.call-start = ((), (), s32[]{:S(2)}) async-start(), calls=%async_computation.3 | async-start | bytes 131072
  94.8 2.7 copy-start
  122.4 191.6 %reduce-scatter.2.cloned.1.call-start = ((), (), s32[]{:S(2)}) async-start(), calls=%async_computation.2 | async-start | bytes 14155776 | tf_op jit(solution)/shard_map/reduce_scatter | solution.py:94
Sparse Core Ops, SparseCore 0:
  9.6 67.4 all-gather.2
  122.5 38.7 all-reduce.2
  184.7 129.2 reduce-scatter.1
where the time goes:
time: 324 us
  waiting for transfers between devices  229 us (71%)
  matrix products  38.6 us (12%)
  blocking collectives  21.8 us (7%)
  other arithmetic  14.9 us (5%)
  between operations  14.5 us (4%)
  local copies, waits for them, and re-layouts  4.82 us (1%)
    reduce_scatter x1, waiting for transfers between devices, on_device(): lax.psum_scatter(lax.dot_general(w_rows, dlogits, (((1,), (1,)), ((), ())...  129 us
    all_gather x1, waiting for transfers between devices, on_device(): lax.all_gather(tokens, 'vocab', axis=1, tiled=True)  62.9 us
    unnamed x4, waiting for transfers between devices  36.3 us
    dot_general x1, matrix products, on_device(): lax.dot_general(w_rows, dlogits, (((1,), (1,)), ((), ())), preferred_elem...  19.4 us
    dot_general x1, matrix products, on_device(): jnp.dot(lax.all_gather(tokens, 'vocab', axis=1, tiled=True), w_rows, pref...  17.7 us
    psum x1, blocking collectives, on_device(): scores = lax.psum(exact_dot(q_pooled, p_every.T), 'vocab') / score_div  13.6 us
    all_gather x1, blocking collectives, on_device(): p_every = lax.all_gather(p_pooled, 'dp', axis=0, tiled=True)  8.21 us
  transfers between devices with their start and end apart: 3, of which 3 were waited for; matrix products, arithmetic and copies ran while one was open for 2% of the time, Pallas kernels for 0%

commit v1 on v0

v1 whole, which is shorter than its diff:
```python
import functools

import jax
import jax.numpy as jnp
from jax import lax
from jax.experimental import pallas as pl
from jax.experimental.pallas import tpu as pltpu
from jax.sharding import PartitionSpec as P

sharpness = 0.2
score_div = 16.0
loss_scale = 65536.0
lanes = 128
low = -1e30
MESH = pl.DeviceIdType.MESH


def nt_dot(left, right):
    return lax.dot_general(
        left, right, (((1,), (1,)), ((), ())), preferred_element_type=jnp.float32
    )


def kernel(
    cfg,
    q_hbm, p_hbm, w_hbm, q_mask, p_mask, picked_ref,
    gq_ref, gp_ref, loss_ref,
    w, xg, acc, dl, in_l, in_r, out_l, out_r, sib_in, sib_out, own, part,
    smooth, total, coef, pooled, scores, dscores, losses,
    load_sem, w_sem, recv1, send1, recv_p, send_p, recv_s, send_s,
    recv_l, recv_r, send_l, send_r, recv_sib, send_sib,
):
    G, V, B, R, F, C, q_count, p_count, q_len = cfg
    L = V // 2
    passages = G * p_count
    g = lax.axis_index("dp")
    me = lax.axis_index("vocab")
    c = lax.rem(me, 2)
    i = lax.div(me, 2)
    sib = me + 1 - 2 * c
    has_left, has_right = i > 0, i < L - 1

    loads = []
    for b in range(B):
        src = q_hbm if b == 0 else p_hbm.at[pl.ds((b - 1) * R, R)]
        loads.append(pltpu.make_async_copy(src, xg.at[me, b], load_sem.at[b]))
    for load in loads:
        load.start()
    w_load = pltpu.make_async_copy(w_hbm, w, w_sem)
    w_load.start()

    barrier = pltpu.get_barrier_semaphore()
    for k in range(1, V):
        pl.semaphore_signal(
            barrier, inc=1, device_id={"vocab": lax.rem(me + k, V)}, device_id_type=MESH
        )
    for k in range(1, G):
        pl.semaphore_signal(
            barrier, inc=1, device_id={"dp": lax.rem(g + k, G)}, device_id_type=MESH
        )
    pl.semaphore_wait(barrier, V - 1 + G - 1)
    for load in loads:
        load.wait()

    def hop(v, b, way, target):
        return pltpu.make_async_remote_copy(
            src_ref=xg.at[v, b],
            dst_ref=xg.at[v, b],
            send_sem=send1.at[way, v, b],
            recv_sem=recv1.at[v, b],
            device_id={"vocab": target},
            device_id_type=MESH,
        )

    def send_own(b):
        @pl.when(has_right)
        def _():
            hop(me, b, 0, me + 2).start()

        @pl.when(has_left)
        def _():
            hop(me, b, 1, me - 2).start()

        hop(me, b, 2, sib).start()

    send_own(0)
    acc[...] = jnp.zeros_like(acc)
    pooled[g] = jnp.zeros(pooled.shape[1:], jnp.float32)
    w_load.wait()

    tile = min(512, C)

    def mm1(v, b):
        def body(n, carry):
            cols = pl.ds(pl.multiple_of(n * tile, tile), tile)
            rows = pl.ds(pl.multiple_of(v * F, F), F)
            acc[b, :, cols] += jnp.dot(
                xg[v, b], w[rows, cols], preferred_element_type=jnp.float32
            )
            return carry

        lax.fori_loop(0, C // tile, body, 0)

    ptile = min(256, C)

    def pool(b):
        if b == 0:
            seqs = [(k, k * q_len, q_len, q_mask, k) for k in range(q_count)]
        else:
            seqs = [(q_count + b - 1, 0, R, p_mask, b - 1)]
        for row, first, length, mask, at in seqs:
            live_len = jnp.sum(
                mask[pl.ds(at, 1), :].astype(jnp.float32), axis=1, keepdims=True
            )

            def body(n, carry, row=row, first=first, length=length, live_len=live_len):
                cols = pl.ds(pl.multiple_of(n * ptile, ptile), ptile)
                place = lax.broadcasted_iota(jnp.int32, (length, ptile), 0)
                live = place.astype(jnp.float32) < live_len
                x = jnp.where(live, acc[b, pl.ds(first, length), cols] * (1.0 / sharpness), low)
                top = jnp.max(x, axis=0, keepdims=True)
                e = jnp.where(live, jnp.exp(x - top), 0.0)
                acc[b, pl.ds(first, length), cols] = e
                s = jnp.sum(e, axis=0, keepdims=True)
                sm = sharpness * (top + jnp.log(s))
                smooth[row, :, cols] = sm
                total[row, :, cols] = s
                pooled[g, pl.ds(row, 1), cols] = jnp.log1p(jnp.maximum(sm, 0.0))
                return carry

            lax.fori_loop(0, C // ptile, body, 0)

    def gather_step(s, carry):
        b, h = lax.div(s, L), lax.rem(s, L)
        main = s < B * L
        left, right = i - h, i + h
        from_left = jnp.logical_and(main, left >= 0)
        from_right = jnp.logical_and(main, jnp.logical_and(right < L, h > 0))

        @pl.when(jnp.logical_and(h == 0, b + 1 < B))
        def _():
            send_own(b + 1)

        @pl.when(jnp.logical_and(from_left, h > 0))
        def _():
            v = 2 * left + c
            hop(v, b, 0, sib).wait_recv()

            @pl.when(has_right)
            def _():
                hop(v, b, 0, me + 2).start()

            hop(v, b, 2, sib).start()

        @pl.when(from_right)
        def _():
            v = 2 * right + c
            hop(v, b, 1, sib).wait_recv()

            @pl.when(has_left)
            def _():
                hop(v, b, 1, me - 2).start()

            hop(v, b, 2, sib).start()

        @pl.when(from_left)
        def _():
            mm1(2 * left + c, b)

        @pl.when(from_right)
        def _():
            mm1(2 * right + c, b)

        t = jnp.maximum(s - 1, 0)
        b1, h1 = lax.div(t, L), lax.rem(t, L)
        left1, right1 = i - h1, i + h1

        @pl.when(jnp.logical_and(s > 0, left1 >= 0))
        def _():
            v = 2 * left1 + 1 - c
            hop(v, b1, 2, sib).wait_recv()
            mm1(v, b1)

        @pl.when(jnp.logical_and(s > 0, jnp.logical_and(right1 < L, h1 > 0)))
        def _():
            v = 2 * right1 + 1 - c
            hop(v, b1, 2, sib).wait_recv()
            mm1(v, b1)

        for done in range(B):
            @pl.when(s == (done + 1) * L)
            def _(done=done):
                pool(done)

        return carry

    lax.fori_loop(0, B * L + 1, gather_step, 0)

    def pooled_copy(group, k):
        return pltpu.make_async_remote_copy(
            src_ref=pooled.at[group],
            dst_ref=pooled.at[group],
            send_sem=send_p.at[k],
            recv_sem=recv_p.at[group],
            device_id={"dp": lax.rem(g + k, G)},
            device_id_type=MESH,
        )

    for k in range(1, G):
        pooled_copy(g, k).start()
    for k in range(1, G):
        pooled_copy(lax.rem(g + k, G), k).wait_recv()

    lane = lax.broadcasted_iota(jnp.int32, (8, lanes), 1)
    blocks = [jnp.zeros((8, lanes), jnp.float32) for _ in range(G)]
    for p in range(passages):
        row = q_count + p % p_count
        vector = pooled[p // p_count, row : row + 1, :]
        for k in range(G):
            value = jnp.sum(pooled[k] * vector, axis=1, keepdims=True)
            blocks[k] = jnp.where(lane == p, value, blocks[k])
    for k in range(G):
        scores[me, k] = blocks[k]

    def score_copy(v, k):
        return pltpu.make_async_remote_copy(
            src_ref=scores.at[v],
            dst_ref=scores.at[v],
            send_sem=send_s.at[k],
            recv_sem=recv_s.at[v],
            device_id={"vocab": lax.rem(me + k, V)},
            device_id_type=MESH,
        )

    for k in range(1, V):
        score_copy(me, k).start()
    for k in range(1, V):
        score_copy(lax.rem(me + k, V), k).wait_recv()

    row_at = lax.broadcasted_iota(jnp.int32, (8, lanes), 0)
    valid = jnp.logical_and(lane < passages, row_at < q_count)
    for k in range(G):
        sc = scores[0, k]
        for v in range(1, V):
            sc = sc + scores[v, k]
        sc = sc / score_div
        masked = jnp.where(lane < passages, sc, low)
        top = jnp.max(masked, axis=1, keepdims=True)
        lse = top + jnp.log(
            jnp.sum(jnp.where(lane < passages, jnp.exp(masked - top), 0.0), axis=1, keepdims=True)
        )
        hot = picked_ref[k]
        losses[k] = lse - jnp.sum(jnp.where(lane < passages, sc, 0.0) * hot, axis=1, keepdims=True) + jnp.zeros_like(sc)
        dscores[k] = jnp.where(
            valid, (jnp.exp(masked - lse) - hot) * (loss_scale / (G * q_count)), 0.0
        )
    loss_ref[...] = losses[g]

    mine = dscores[g]
    dq = jnp.zeros((8, C), jnp.float32)
    for p in range(passages):
        row = q_count + p % p_count
        dq = dq + mine[:, p : p + 1] * pooled[p // p_count, row : row + 1, :]

    def factor(row, dpool):
        sm = smooth[row]
        gate = jnp.where(sm > 0, 1.0 / (1.0 + jnp.maximum(sm, 0.0)), 0.0)
        coef[row] = dpool * (1.0 / score_div) * gate / total[row]

    for k in range(q_count):
        factor(k, dq[k : k + 1, :])
    for k in range(p_count):
        dp = jnp.zeros((8, C), jnp.float32)
        for group in range(G):
            column = jnp.sum(
                jnp.where(lane == g * p_count + k, dscores[group], 0.0), axis=1, keepdims=True
            )
            dp = dp + column * pooled[group]
        factor(q_count + k, jnp.sum(dp, axis=0, keepdims=True))

    def make_dl(b):
        if b == 0:
            seqs = [(k, k * q_len, q_len) for k in range(q_count)]
        else:
            seqs = [(q_count + b - 1, 0, R)]
        for row, first, length in seqs:
            def body(n, carry, row=row, first=first, length=length):
                cols = pl.ds(pl.multiple_of(n * ptile, ptile), ptile)
                dl[b, pl.ds(first, length), cols] = (
                    acc[b, pl.ds(first, length), cols] * coef[row, :, cols]
                ).astype(jnp.bfloat16)
                return carry

            lax.fori_loop(0, C // ptile, body, 0)

    ftile = min(256, F)

    def mm2(v, b, store):
        def body(n, carry):
            at = pl.multiple_of(n * ftile, ftile)
            rows = pl.ds(pl.multiple_of(v * F + at, ftile), ftile)
            store(pl.ds(at, ftile), nt_dot(dl[b], w[rows, :]))
            return carry

        lax.fori_loop(0, F // ftile, body, 0)

    def sib_copy(b, j):
        return pltpu.make_async_remote_copy(
            src_ref=sib_out.at[b, j], dst_ref=sib_in.at[b, j],
            send_sem=send_sib.at[b, j], recv_sem=recv_sib.at[b, j],
            device_id={"vocab": sib}, device_id_type=MESH,
        )

    def right_copy(b, d):
        return pltpu.make_async_remote_copy(
            src_ref=out_r.at[b, d], dst_ref=in_l.at[b, d],
            send_sem=send_r.at[b, d], recv_sem=recv_l.at[b, d],
            device_id={"vocab": me + 2}, device_id_type=MESH,
        )

    def left_copy(b, d):
        return pltpu.make_async_remote_copy(
            src_ref=out_l.at[b, d], dst_ref=in_r.at[b, d],
            send_sem=send_l.at[b, d], recv_sem=recv_r.at[b, d],
            device_id={"vocab": me - 2}, device_id_type=MESH,
        )

    def for_sibling(j, b):
        def store(cols, value):
            sib_out[b, j, :, cols] = value.astype(jnp.bfloat16)

        mm2(2 * j + 1 - c, b, store)
        sib_copy(b, j).start()

    def for_me(j, b, way):
        def store(cols, value):
            part[way, :, cols] = value

        mm2(2 * j + c, b, store)

    def scatter_step(s, carry):
        b, d = lax.div(s, L), L - 1 - lax.rem(s, L)
        for block in range(B):
            @pl.when(s == block * L)
            def _(block=block):
                make_dl(block)

        right, left = i + d, i - d
        go_right = right < L
        go_left = jnp.logical_and(left >= 0, d > 0)

        @pl.when(go_right)
        def _():
            for_sibling(right, b)

        @pl.when(go_left)
        def _():
            for_sibling(left, b)

        @pl.when(jnp.logical_and(go_right, d > 0))
        def _():
            for_me(right, b, 0)

        @pl.when(go_left)
        def _():
            for_me(left, b, 1)

        @pl.when(d == 0)
        def _():
            def store(cols, value):
                own[b, :, cols] = value

            mm2(me, b, store)

        @pl.when(jnp.logical_and(go_right, d > 0))
        def _():
            sib_copy(b, right).wait_recv()
            part[0] += sib_in[b, right].astype(jnp.float32)

            @pl.when(has_left)
            def _():
                right_copy(b, d).wait_recv()
                part[0] += in_l[b, d].astype(jnp.float32)

            out_r[b, d - 1] = part[0].astype(jnp.bfloat16)
            right_copy(b, d - 1).start()

        @pl.when(go_left)
        def _():
            sib_copy(b, left).wait_recv()
            part[1] += sib_in[b, left].astype(jnp.float32)

            @pl.when(has_right)
            def _():
                left_copy(b, d).wait_recv()
                part[1] += in_r[b, d].astype(jnp.float32)

            out_l[b, d - 1] = part[1].astype(jnp.bfloat16)
            left_copy(b, d - 1).start()

        return carry

    lax.fori_loop(0, B * L, scatter_step, 0)

    for b in range(B):
        sib_copy(b, i).wait_recv()
        own[b] += sib_in[b, i].astype(jnp.float32)

        @pl.when(has_left)
        def _():
            right_copy(b, 0).wait_recv()
            own[b] += in_l[b, 0].astype(jnp.float32)

        @pl.when(has_right)
        def _():
            left_copy(b, 0).wait_recv()
            own[b] += in_r[b, 0].astype(jnp.float32)

        if b == 0:
            gq_ref[...] = own[b].astype(jnp.bfloat16)
        else:
            gp_ref[pl.ds((b - 1) * R, R), :] = own[b].astype(jnp.bfloat16)

    for k in range(1, G):
        pooled_copy(g, k).wait_send()
    for k in range(1, V):
        score_copy(me, k).wait_send()

    def drain(s, carry):
        b, j = lax.div(s, L), lax.rem(s, L)
        v = 2 * j + c
        hop(v, b, 2, sib).wait_send()
        sib_copy(b, j).wait_send()

        @pl.when(jnp.logical_and(has_right, j <= i))
        def _():
            hop(v, b, 0, me + 2).wait_send()

        @pl.when(jnp.logical_and(has_left, j >= i))
        def _():
            hop(v, b, 1, me - 2).wait_send()

        @pl.when(jnp.logical_and(j > 0, i + j < L))
        def _():
            right_copy(b, j - 1).wait_send()

        @pl.when(jnp.logical_and(j > 0, i - j >= 0))
        def _():
            left_copy(b, j - 1).wait_send()

        return carry

    lax.fori_loop(0, B * L, drain, 0)


def on_device(G, V, query_hidden, passage_hidden, head_weight, query_mask, passage_mask, positive):
    q_count, q_len, F = query_hidden.shape
    p_count, p_len, _ = passage_hidden.shape
    D, C = head_weight.shape
    R = p_len
    assert q_count * q_len == R and q_count + p_count <= 8
    B = 1 + p_count
    L = V // 2
    hot = positive[:, None] == jnp.arange(lanes, dtype=jnp.int32)[None, :]
    picked = jnp.pad(
        hot.astype(jnp.float32).reshape(G, q_count, lanes), ((0, 0), (0, 8 - q_count), (0, 0))
    )
    cfg = (G, V, B, R, F, C, q_count, p_count, q_len)
    seqs = q_count + p_count
    bf, f32, dma = jnp.bfloat16, jnp.float32, pltpu.SemaphoreType.DMA
    vmem, anywhere = pl.BlockSpec(memory_space=pltpu.VMEM), pl.BlockSpec(memory_space=pl.ANY)
    line = pltpu.VMEM((B, L - 1, R, F), bf)
    gq, gp, loss = pl.pallas_call(
        functools.partial(kernel, cfg),
        out_shape=(
            jax.ShapeDtypeStruct((R, F), bf),
            jax.ShapeDtypeStruct((p_count * R, F), bf),
            jax.ShapeDtypeStruct((8, lanes), f32),
        ),
        in_specs=[anywhere, anywhere, anywhere, vmem, vmem, vmem],
        out_specs=(vmem, vmem, vmem),
        scratch_shapes=[
            pltpu.VMEM((D, C), bf),
            pltpu.VMEM((V, B, R, F), bf),
            pltpu.VMEM((B, R, C), f32),
            pltpu.VMEM((B, R, C), bf),
            line, line, line, line,
            pltpu.VMEM((B, L, R, F), bf),
            pltpu.VMEM((B, L, R, F), bf),
            pltpu.VMEM((B, R, F), f32),
            pltpu.VMEM((2, R, F), f32),
            pltpu.VMEM((seqs, 1, C), f32),
            pltpu.VMEM((seqs, 1, C), f32),
            pltpu.VMEM((seqs, 1, C), f32),
            pltpu.VMEM((G, 8, C), f32),
            pltpu.VMEM((V, G, 8, lanes), f32),
            pltpu.VMEM((G, 8, lanes), f32),
            pltpu.VMEM((G, 8, lanes), f32),
            dma((B,)),
            dma,
            dma((V, B)),
            dma((3, V, B)),
            dma((G,)),
            dma((G,)),
            dma((V,)),
            dma((V,)),
            dma((B, L - 1)),
            dma((B, L - 1)),
            dma((B, L - 1)),
            dma((B, L - 1)),
            dma((B, L)),
            dma((B, L)),
        ],
        compiler_params=pltpu.CompilerParams(
            collective_id=0, has_side_effects=True, vmem_limit_bytes=60 * 1024 * 1024
        ),
    )(
        query_hidden.reshape(R, F),
        passage_hidden.reshape(p_count * R, F),
        head_weight,
        query_mask,
        passage_mask,
        picked,
    )
    return (
        gq.reshape(query_hidden.shape),
        gp.reshape(passage_hidden.shape),
        loss[:q_count, 0],
    )


def solution(mesh):
    return jax.shard_map(
        functools.partial(on_device, mesh.shape["dp"], mesh.shape["vocab"]),
        mesh=mesh,
        in_specs=(
            P("dp", None, "vocab"),
            P("dp", None, "vocab"),
            P(None, "vocab"),
            P("dp", None),
            P("dp", None),
            P(),
        ),
        out_specs=(P("dp", None, "vocab"), P("dp", None, "vocab"), P("dp")),
        check_vma=False,
    )
```

time: 324 us -> 147 us (0.45)
  waiting for transfers between devices: 229 us -> 0 us
  Pallas kernels: 0 us -> 140 us
  matrix products: 38.6 us -> 0 us
  blocking collectives: 21.8 us -> 0 us
  other arithmetic: 14.9 us -> 0.69 us
  between operations: 14.5 us -> 0.64 us
    pallas_call x0 -> x1, Pallas kernels: none -> 140 us  [on_device(): pl.pallas_call(functools.partial(kernel, cfg), out_shape=(jax.ShapeDtypeS...]
    reduce_scatter x1 -> x0, waiting for transfers between devices: 129 us -> none  [on_device(): lax.psum_scatter(lax.dot_general(w_rows, dlogits, (((1,), (1,)), ((), ())...]
    all_gather x1 -> x0, waiting for transfers between devices: 62.9 us -> none  [on_device(): lax.all_gather(tokens, 'vocab', axis=1, tiled=True)]
    dot_general x5 -> x0, matrix products: 38.6 us -> none  [the longest x1 19.4 us: on_device(): lax.dot_general(w_rows, dlogits, (((1,), (1,)), ((), ())), preferred_elem...]
    unnamed x4 -> x0, waiting for transfers between devices: 36.3 us -> none
    psum x1 -> x0, blocking collectives: 13.6 us -> none  [on_device(): scores = lax.psum(exact_dot(q_pooled, p_every.T), 'vocab') / score_div]
    all_gather x1 -> x0, blocking collectives: 8.21 us -> none  [on_device(): p_every = lax.all_gather(p_pooled, 'dp', axis=0, tiled=True)]
    convert_element_type x3 -> x0, other arithmetic: 6.62 us -> none  [the longest x2 5.12 us: token_grads(): dlogits = (share * dsmooth[:, None, :]).astype(jnp.bfloat16)]
  transfers between devices with their start and end apart: 3 -> 0, of which waited for: 3 -> 0; matrix products, arithmetic and copies ran while one was open for 2% -> 0% of each run, Pallas kernels for 0% -> 0%
where the time goes in v1:
time: 147 us
  Pallas kernels  140 us (95%)
  local copies, waits for them, and re-layouts  5.58 us (4%)
    pallas_call x1, Pallas kernels, on_device(): pl.pallas_call(functools.partial(kernel, cfg), out_shape=(jax.ShapeDtypeS...  140 us
    unnamed x2, local copies, waits for them, and re-layouts  3.54 us

profile of v1, /device:TPU:0, one launch (start us, length us, event | category | flops | bytes accessed | tf_op | source)
XLA Modules:
  0.0 146.8 jit_solution(6412984645265718473)
XLA Ops:
  0.6 0.7 eq.16
  1.4 0.1 iota_compare_fusion
  1.4 0.6 pad_convert_fusion.picked_ref
  2.1 139.9 %shard_map.85 = (bf16[256,512]{1,0:T(8,128)(2,1)}, bf16[512,512]{1,0:T(8,128)(2,1)}, f32[8,128]{1,0:T(8,128)}) custom-call(bf16[256,512]{1,0:T(8,128)(2,1)} %bitcast.6, bf16[512,512]{1,0:T(8,128)(2,1)} %bitcast.4, bf16[4096,2048]{1,0:T(8,128)(2,1)} %w_hbm.1, s32[2,128]{1,0:T(2,128)} %q_mask.1, s32[2,256]{1,0:T(2,128)} %p_mask.1, ...), custom_call_target="tpu_custom_call" | custom-call | tf_op jit(solution)/shard_map/pallas_call | solution.py:473
  141.9 1.3 slice_reduce_fusion
  143.2 1.7 %copy.11 = bf16[2,128,512]{2,1,0:T(8,128)(2,1)} copy(bf16[2,128,512]{2,1,0:T(8,128)(2,1)} %bitcast.7) | data formatting | bytes 524288
  144.9 1.9 %copy.12 = bf16[2,256,512]{2,1,0:T(8,128)(2,1)} copy(bf16[2,256,512]{2,1,0:T(8,128)(2,1)} %bitcast.5) | data formatting | bytes 1048576

commit v2 on v1

--- a/solution.py
+++ b/solution.py
@@ -24,8 +24,8 @@
 def kernel(
     cfg,
     q_hbm, p_hbm, w_hbm, q_mask, p_mask, picked_ref,
-    gq_ref, gp_ref, loss_ref,
-    w, xg, acc, dl, in_l, in_r, out_l, out_r, sib_in, sib_out, own, part,
+    out_ref, loss_ref,
+    w, xg, acc, dl, in_l, in_r, out_l, out_r, sib_in, sib_out, part,
     smooth, total, coef, pooled, scores, dscores, losses,
     load_sem, w_sem, recv1, send1, recv_p, send_p, recv_s, send_s,
     recv_l, recv_r, send_l, send_r, recv_sib, send_sib,
@@ -278,15 +278,15 @@
             dp = dp + column * pooled[group]
         factor(q_count + k, jnp.sum(dp, axis=0, keepdims=True))
 
-    def make_dl(b):
+    for b in range(B):
         if b == 0:
             seqs = [(k, k * q_len, q_len) for k in range(q_count)]
         else:
             seqs = [(q_count + b - 1, 0, R)]
         for row, first, length in seqs:
-            def body(n, carry, row=row, first=first, length=length):
+            def body(n, carry, b=b, row=row, first=first, length=length):
                 cols = pl.ds(pl.multiple_of(n * ptile, ptile), ptile)
-                dl[b, pl.ds(first, length), cols] = (
+                dl[pl.ds(b * R + first, length), cols] = (
                     acc[b, pl.ds(first, length), cols] * coef[row, :, cols]
                 ).astype(jnp.bfloat16)
                 return carry
@@ -295,19 +295,19 @@
 
     ftile = min(256, F)
 
-    def mm2(v, b, store):
+    def mm2(v, store):
         def body(n, carry):
             at = pl.multiple_of(n * ftile, ftile)
             rows = pl.ds(pl.multiple_of(v * F + at, ftile), ftile)
-            store(pl.ds(at, ftile), nt_dot(dl[b], w[rows, :]))
+            store(pl.ds(at, ftile), nt_dot(dl[...], w[rows, :]))
             return carry
 
         lax.fori_loop(0, F // ftile, body, 0)
 
-    def sib_copy(b, j):
+    def sib_copy(j):
         return pltpu.make_async_remote_copy(
-            src_ref=sib_out.at[b, j], dst_ref=sib_in.at[b, j],
-            send_sem=send_sib.at[b, j], recv_sem=recv_sib.at[b, j],
+            src_ref=sib_out.at[j], dst_ref=sib_in.at[j],
+            send_sem=send_sib.at[j], recv_sem=recv_sib.at[j],
             device_id={"vocab": sib}, device_id_type=MESH,
         )
 
@@ -325,101 +325,121 @@
             device_id={"vocab": me - 2}, device_id_type=MESH,
         )
 
-    def for_sibling(j, b):
+    def for_sibling(j):
         def store(cols, value):
-            sib_out[b, j, :, cols] = value.astype(jnp.bfloat16)
-
-        mm2(2 * j + 1 - c, b, store)
-        sib_copy(b, j).start()
-
-    def for_me(j, b, way):
+            sib_out[j, :, cols] = value.astype(jnp.bfloat16)
+
+        mm2(2 * j + 1 - c, store)
+        sib_copy(j).start()
+
+    def for_me(j, way):
         def store(cols, value):
             part[way, :, cols] = value
 
-        mm2(2 * j + c, b, store)
+        mm2(2 * j + c, store)
+
+    def pass_on(way, j, b, d, more, copy, arrived, out):
+        rows = pl.ds(b * R, R)
+
+        @pl.when(more)
+        def _():
+            copy(b, d).wait_recv()
+            out[b, d - 1] = (
+                part[way, rows]
+                + sib_in[j, rows].astype(jnp.float32)
+                + arrived[b, d].astype(jnp.float32)
+            ).astype(jnp.bfloat16)
+
+        @pl.when(jnp.logical_not(more))
+        def _():
+            out[b, d - 1] = (
+                part[way, rows] + sib_in[j, rows].astype(jnp.float32)
+            ).astype(jnp.bfloat16)
+
+        copy(b, d - 1).start()
 
     def scatter_step(s, carry):
-        b, d = lax.div(s, L), L - 1 - lax.rem(s, L)
-        for block in range(B):
-            @pl.when(s == block * L)
-            def _(block=block):
-                make_dl(block)
-
+        d = L - 1 - s
         right, left = i + d, i - d
         go_right = right < L
         go_left = jnp.logical_and(left >= 0, d > 0)
+        on_right = jnp.logical_and(go_right, d > 0)
 
         @pl.when(go_right)
         def _():
-            for_sibling(right, b)
+            for_sibling(right)
 
         @pl.when(go_left)
         def _():
-            for_sibling(left, b)
-
-        @pl.when(jnp.logical_and(go_right, d > 0))
-        def _():
-            for_me(right, b, 0)
+            for_sibling(left)
+
+        @pl.when(go_right)
+        def _():
+            for_me(right, 0)
 
         @pl.when(go_left)
         def _():
-            for_me(left, b, 1)
-
-        @pl.when(d == 0)
-        def _():
-            def store(cols, value):
-                own[b, :, cols] = value
-
-            mm2(me, b, store)
-
-        @pl.when(jnp.logical_and(go_right, d > 0))
-        def _():
-            sib_copy(b, right).wait_recv()
-            part[0] += sib_in[b, right].astype(jnp.float32)
-
-            @pl.when(has_left)
-            def _():
-                right_copy(b, d).wait_recv()
-                part[0] += in_l[b, d].astype(jnp.float32)
-
-            out_r[b, d - 1] = part[0].astype(jnp.bfloat16)
-            right_copy(b, d - 1).start()
+            for_me(left, 1)
+
+        @pl.when(on_right)
+        def _():
+            sib_copy(right).wait_recv()
 
         @pl.when(go_left)
         def _():
-            sib_copy(b, left).wait_recv()
-            part[1] += sib_in[b, left].astype(jnp.float32)
-
-            @pl.when(has_right)
-            def _():
-                left_copy(b, d).wait_recv()
-                part[1] += in_r[b, d].astype(jnp.float32)
-
-            out_l[b, d - 1] = part[1].astype(jnp.bfloat16)
-            left_copy(b, d - 1).start()
+            sib_copy(left).wait_recv()
+
+        for b in range(B):
+            @pl.when(on_right)
+            def _(b=b):
+                pass_on(0, right, b, d, has_left, right_copy, in_l, out_r)
+
+            @pl.when(go_left)
+            def _(b=b):
+                pass_on(1, left, b, d, has_right, left_copy, in_r, out_l)
 
         return carry
 
-    lax.fori_loop(0, B * L, scatter_step, 0)
-
+    lax.fori_loop(0, L, scatter_step, 0)
+
+    sib_copy(i).wait_recv()
     for b in range(B):
-        sib_copy(b, i).wait_recv()
-        own[b] += sib_in[b, i].astype(jnp.float32)
-
-        @pl.when(has_left)
+        rows = pl.ds(b * R, R)
+
+        @pl.when(jnp.logical_and(has_left, has_right))
         def _():
             right_copy(b, 0).wait_recv()
-            own[b] += in_l[b, 0].astype(jnp.float32)
-
-        @pl.when(has_right)
-        def _():
             left_copy(b, 0).wait_recv()
-            own[b] += in_r[b, 0].astype(jnp.float32)
-
-        if b == 0:
-            gq_ref[...] = own[b].astype(jnp.bfloat16)
-        else:
-            gp_ref[pl.ds((b - 1) * R, R), :] = own[b].astype(jnp.bfloat16)
+            out_ref[rows, :] = (
+                part[0, rows]
+                + sib_in[i, rows].astype(jnp.float32)
+                + in_l[b, 0].astype(jnp.float32)
+                + in_r[b, 0].astype(jnp.float32)
+            ).astype(jnp.bfloat16)
+
+        @pl.when(jnp.logical_and(has_left, jnp.logical_not(has_right)))
+        def _():
+            right_copy(b, 0).wait_recv()
+            out_ref[rows, :] = (
+                part[0, rows]
+                + sib_in[i, rows].astype(jnp.float32)
+                + in_l[b, 0].astype(jnp.float32)
+            ).astype(jnp.bfloat16)
+
+        @pl.when(jnp.logical_and(jnp.logical_not(has_left), has_right))
+        def _():
+            left_copy(b, 0).wait_recv()
+            out_ref[rows, :] = (
+                part[0, rows]
+                + sib_in[i, rows].astype(jnp.float32)
+                + in_r[b, 0].astype(jnp.float32)
+            ).astype(jnp.bfloat16)
+
+        @pl.when(jnp.logical_not(jnp.logical_or(has_left, has_right)))
+        def _():
+            out_ref[rows, :] = (
+                part[0, rows] + sib_in[i, rows].astype(jnp.float32)
+            ).astype(jnp.bfloat16)
 
     for k in range(1, G):
         pooled_copy(g, k).wait_send()
@@ -430,7 +450,6 @@
         b, j = lax.div(s, L), lax.rem(s, L)
         v = 2 * j + c
         hop(v, b, 2, sib).wait_send()
-        sib_copy(b, j).wait_send()
 
         @pl.when(jnp.logical_and(has_right, j <= i))
         def _():
@@ -451,6 +470,8 @@
         return carry
 
     lax.fori_loop(0, B * L, drain, 0)
+    for j in range(L):
+        sib_copy(j).wait_send()
 
 
 def on_device(G, V, query_hidden, passage_hidden, head_weight, query_mask, passage_mask, positive):
@@ -470,25 +491,23 @@
     bf, f32, dma = jnp.bfloat16, jnp.float32, pltpu.SemaphoreType.DMA
     vmem, anywhere = pl.BlockSpec(memory_space=pltpu.VMEM), pl.BlockSpec(memory_space=pl.ANY)
     line = pltpu.VMEM((B, L - 1, R, F), bf)
-    gq, gp, loss = pl.pallas_call(
+    grads, loss = pl.pallas_call(
         functools.partial(kernel, cfg),
         out_shape=(
-            jax.ShapeDtypeStruct((R, F), bf),
-            jax.ShapeDtypeStruct((p_count * R, F), bf),
+            jax.ShapeDtypeStruct((B * R, F), bf),
             jax.ShapeDtypeStruct((8, lanes), f32),
         ),
         in_specs=[anywhere, anywhere, anywhere, vmem, vmem, vmem],
-        out_specs=(vmem, vmem, vmem),
+        out_specs=(vmem, vmem),
         scratch_shapes=[
             pltpu.VMEM((D, C), bf),
             pltpu.VMEM((V, B, R, F), bf),
             pltpu.VMEM((B, R, C), f32),
-            pltpu.VMEM((B, R, C), bf),
+            pltpu.VMEM((B * R, C), bf),
             line, line, line, line,
-            pltpu.VMEM((B, L, R, F), bf),
-            pltpu.VMEM((B, L, R, F), bf),
-            pltpu.VMEM((B, R, F), f32),
-            pltpu.VMEM((2, R, F), f32),
+            pltpu.VMEM((L, B * R, F), bf),
+            pltpu.VMEM((L, B * R, F), bf),
+            pltpu.VMEM((2, B * R, F), f32),
             pltpu.VMEM((seqs, 1, C), f32),
             pltpu.VMEM((seqs, 1, C), f32),
             pltpu.VMEM((seqs, 1, C), f32),
@@ -508,8 +527,8 @@
             dma((B, L - 1)),
             dma((B, L - 1)),
             dma((B, L - 1)),
-            dma((B, L)),
-            dma((B, L)),
+            dma((L,)),
+            dma((L,)),
         ],
         compiler_params=pltpu.CompilerParams(
             collective_id=0, has_side_effects=True, vmem_limit_bytes=60 * 1024 * 1024
@@ -523,8 +542,8 @@
         picked,
     )
     return (
-        gq.reshape(query_hidden.shape),
-        gp.reshape(passage_hidden.shape),
+        grads[:R].reshape(query_hidden.shape),
+        grads[R:].reshape(passage_hidden.shape),
         loss[:q_count, 0],
     )
 

time: 147 us -> 144 us (0.980)
  Pallas kernels: 140 us -> 137 us
    slice x0 -> x2, local copies, waits for them, and re-layouts: none -> 3.54 us  [the longest x1 1.87 us: on_device(): grads[R:].reshape(passage_hidden.shape)]
    unnamed x2 -> x0, local copies, waits for them, and re-layouts: 3.54 us -> none
    pallas_call x1, Pallas kernels: 140 us -> 137 us  [on_device(): pl.pallas_call(functools.partial(kernel, cfg), out_shape=(jax.ShapeDtypeS...]
where the time goes in v2:
time: 144 us
  Pallas kernels  137 us (95%)
  local copies, waits for them, and re-layouts  5.58 us (4%)
    pallas_call x1, Pallas kernels, on_device(): pl.pallas_call(functools.partial(kernel, cfg), out_shape=(jax.ShapeDtypeS...  137 us

profile of v2, /device:TPU:0, one launch (start us, length us, event | category | flops | bytes accessed | tf_op | source)
XLA Modules:
  0.0 143.8 jit_solution(225295659675666564)
XLA Ops:
  0.6 0.7 eq.16
  1.4 0.1 iota_compare_fusion
  1.4 0.6 pad_convert_fusion.picked_ref
  2.1 136.9 %shard_map.85 = (bf16[768,512]{1,0:T(8,128)(2,1)}, f32[8,128]{1,0:T(8,128)}) custom-call(bf16[256,512]{1,0:T(8,128)(2,1)} %bitcast.6, bf16[512,512]{1,0:T(8,128)(2,1)} %bitcast.4, bf16[4096,2048]{1,0:T(8,128)(2,1)} %w_hbm.1, s32[2,128]{1,0:T(2,128)} %q_mask.1, s32[2,256]{1,0:T(2,128)} %p_mask.1, f32[4,8,128]{2,1,0:T(8,128)} %pad_convert_fusion.picked_ref), custom_call_target="tpu_custom_call" | custom-call | tf_op jit(solution)/shard_map/pallas_call | solution.py:494
  138.9 1.3 slice_reduce_fusion
  140.2 1.7 %slice.9 = bf16[256,512]{1,0:T(8,128)(2,1)} slice(bf16[768,512]{1,0:T(8,128)(2,1)} %get-tuple-element.5), slice={[0:256], [0:512]} | slice | bytes 524288 | tf_op jit(solution)/shard_map/slice | solution.py:545
  141.9 1.9 %slice.10 = bf16[512,512]{1,0:T(8,128)(2,1)} slice(bf16[768,512]{1,0:T(8,128)(2,1)} %get-tuple-element.5), slice={[256:768], [0:512]} | slice | bytes 1048576 | tf_op jit(solution)/shard_map/slice | solution.py:546

commit v3 on v2

--- a/solution.py
+++ b/solution.py
@@ -295,19 +295,22 @@
 
     ftile = min(256, F)
 
-    def mm2(v, store):
+    everything = pl.ds(0, B * R)
+
+    def mm2(v, store, tokens=everything):
         def body(n, carry):
             at = pl.multiple_of(n * ftile, ftile)
             rows = pl.ds(pl.multiple_of(v * F + at, ftile), ftile)
-            store(pl.ds(at, ftile), nt_dot(dl[...], w[rows, :]))
+            store(pl.ds(at, ftile), nt_dot(dl[tokens, :], w[rows, :]))
             return carry
 
         lax.fori_loop(0, F // ftile, body, 0)
 
-    def sib_copy(j):
+    def sib_copy(b, j):
+        rows = pl.ds(b * R if isinstance(b, int) else pl.multiple_of(b * R, R), R)
         return pltpu.make_async_remote_copy(
-            src_ref=sib_out.at[j], dst_ref=sib_in.at[j],
-            send_sem=send_sib.at[j], recv_sem=recv_sib.at[j],
+            src_ref=sib_out.at[j, rows], dst_ref=sib_in.at[j, rows],
+            send_sem=send_sib.at[b, j], recv_sem=recv_sib.at[b, j],
             device_id={"vocab": sib}, device_id_type=MESH,
         )
 
@@ -330,7 +333,8 @@
             sib_out[j, :, cols] = value.astype(jnp.bfloat16)
 
         mm2(2 * j + 1 - c, store)
-        sib_copy(j).start()
+        for b in range(B):
+            sib_copy(b, j).start()
 
     def for_me(j, way):
         def store(cols, value):
@@ -340,6 +344,7 @@
 
     def pass_on(way, j, b, d, more, copy, arrived, out):
         rows = pl.ds(b * R, R)
+        sib_copy(b, j).wait_recv()
 
         @pl.when(more)
         def _():
@@ -381,14 +386,6 @@
         def _():
             for_me(left, 1)
 
-        @pl.when(on_right)
-        def _():
-            sib_copy(right).wait_recv()
-
-        @pl.when(go_left)
-        def _():
-            sib_copy(left).wait_recv()
-
         for b in range(B):
             @pl.when(on_right)
             def _(b=b):
@@ -400,11 +397,44 @@
 
         return carry
 
-    lax.fori_loop(0, L, scatter_step, 0)
-
-    sib_copy(i).wait_recv()
+    @pl.when(jnp.logical_or(i == 0, i == L - 1))
+    def _():
+        j = L - 1 - i
+
+        def first(b, carry):
+            rows = pl.ds(pl.multiple_of(b * R, R), R)
+
+            def store_sib(cols, value):
+                sib_out[j, rows, cols] = value.astype(jnp.bfloat16)
+
+            def store_own(cols, value):
+                part[0, rows, cols] = value
+
+            mm2(2 * j + 1 - c, store_sib, rows)
+            sib_copy(b, j).start()
+            mm2(2 * j + c, store_own, rows)
+            sib_copy(b, j).wait_recv()
+            value = (part[0, rows] + sib_in[j, rows].astype(jnp.float32)).astype(jnp.bfloat16)
+
+            @pl.when(i == 0)
+            def _():
+                out_r[b, L - 2] = value
+                right_copy(b, L - 2).start()
+
+            @pl.when(i == L - 1)
+            def _():
+                out_l[b, L - 2] = value
+                left_copy(b, L - 2).start()
+
+            return carry
+
+        lax.fori_loop(0, B, first, 0)
+
+    lax.fori_loop(1, L, scatter_step, 0)
+
     for b in range(B):
         rows = pl.ds(b * R, R)
+        sib_copy(b, i).wait_recv()
 
         @pl.when(jnp.logical_and(has_left, has_right))
         def _():
@@ -450,6 +480,7 @@
         b, j = lax.div(s, L), lax.rem(s, L)
         v = 2 * j + c
         hop(v, b, 2, sib).wait_send()
+        sib_copy(b, j).wait_send()
 
         @pl.when(jnp.logical_and(has_right, j <= i))
         def _():
@@ -470,8 +501,6 @@
         return carry
 
     lax.fori_loop(0, B * L, drain, 0)
-    for j in range(L):
-        sib_copy(j).wait_send()
 
 
 def on_device(G, V, query_hidden, passage_hidden, head_weight, query_mask, passage_mask, positive):
@@ -527,11 +556,11 @@
             dma((B, L - 1)),
             dma((B, L - 1)),
             dma((B, L - 1)),
-            dma((L,)),
-            dma((L,)),
+            dma((B, L)),
+            dma((B, L)),
         ],
         compiler_params=pltpu.CompilerParams(
-            collective_id=0, has_side_effects=True, vmem_limit_bytes=60 * 1024 * 1024
+            collective_id=0, has_side_effects=True, vmem_limit_bytes=56 * 1024 * 1024
         ),
     )(
         query_hidden.reshape(R, F),

time: 144 us -> 142 us (0.986)
  Pallas kernels: 137 us -> 135 us
    pallas_call x1, Pallas kernels: 137 us -> 135 us  [on_device(): pl.pallas_call(functools.partial(kernel, cfg), out_shape=(jax.ShapeDtypeS...]
where the time goes in v3:
time: 142 us
  Pallas kernels  135 us (95%)
  local copies, waits for them, and re-layouts  5.58 us (4%)
    pallas_call x1, Pallas kernels, on_device(): pl.pallas_call(functools.partial(kernel, cfg), out_shape=(jax.ShapeDtypeS...  135 us

profile of v3, /device:TPU:0, one launch (start us, length us, event | category | flops | bytes accessed | tf_op | source)
XLA Modules:
  0.0 142.1 jit_solution(11523298424112163314)
XLA Ops:
  0.6 0.7 eq.16
  1.4 0.1 iota_compare_fusion
  1.4 0.6 pad_convert_fusion.picked_ref
  2.1 135.2 %shard_map.85 = (bf16[768,512]{1,0:T(8,128)(2,1)}, f32[8,128]{1,0:T(8,128)}) custom-call(bf16[256,512]{1,0:T(8,128)(2,1)} %bitcast.6, bf16[512,512]{1,0:T(8,128)(2,1)} %bitcast.4, bf16[4096,2048]{1,0:T(8,128)(2,1)} %w_hbm.1, s32[2,128]{1,0:T(2,128)} %q_mask.1, s32[2,256]{1,0:T(2,128)} %p_mask.1, f32[4,8,128]{2,1,0:T(8,128)} %pad_convert_fusion.picked_ref), custom_call_target="tpu_custom_call" | custom-call | tf_op jit(solution)/shard_map/pallas_call | solution.py:523
  137.3 1.3 slice_reduce_fusion
  138.6 1.7 %slice.9 = bf16[256,512]{1,0:T(8,128)(2,1)} slice(bf16[768,512]{1,0:T(8,128)(2,1)} %get-tuple-element.5), slice={[0:256], [0:512]} | slice | bytes 524288 | tf_op jit(solution)/shard_map/slice | solution.py:574
  140.3 1.9 %slice.10 = bf16[512,512]{1,0:T(8,128)(2,1)} slice(bf16[768,512]{1,0:T(8,128)(2,1)} %get-tuple-element.5), slice={[256:768], [0:512]} | slice | bytes 1048576 | tf_op jit(solution)/shard_map/slice | solution.py:575
